TPU v7x, 512 devices: a whole 4x8x8 slice. The times are simulated.
512 devices in a mesh: dp: 32 (over x, z), hid: 16 (over y, core).
Axes of the slice: x: 4, y: 8, z: 8, core: 2. Of those that a mesh axis runs over, the one named last changes fastest.
Arguments:
- inputs: bfloat16 [8192, 8192], P('dp', 'hid'), may hold values from -6 to 6
- out_grad: bfloat16 [8192, 8192], P('dp', 'hid'), may hold values from -6 to 6
- home_block: int32 [64], P('hid'), may hold values from 0 to 1
- blocks_up: bfloat16 [64, 3, 256, 256], P('hid', None, 'dp'), may hold values from -0.21875 to 0.21875
- blocks_down: bfloat16 [64, 3, 256, 256], P('hid', None, 'dp'), may hold values from -0.15625 to 0.15625
- up_left: bfloat16 [8192, 128], P('hid', 'dp'), may hold values from -0.0625 to 0.0625
- up_right: bfloat16 [128, 16384], P('dp', 'hid'), may hold values from -0.5 to 0.5
- down_left: bfloat16 [16384, 128], P('hid', 'dp'), may hold values from -0.046875 to 0.046875
- down_right: bfloat16 [128, 8192], P('dp', 'hid'), may hold values from -0.5 to 0.5
Outputs:
- outputs: bfloat16 [8192, 8192], P('dp', 'hid')
- input_grad: bfloat16 [8192, 8192], P('dp', 'hid')
- grad_blocks_up: bfloat16 [64, 3, 256, 256], P('hid', None, 'dp')
- grad_blocks_down: bfloat16 [64, 3, 256, 256], P('hid', None, 'dp')
- grad_up_left: bfloat16 [8192, 128], P('hid', 'dp')
- grad_up_right: bfloat16 [128, 16384], P('dp', 'hid')
- grad_down_left: bfloat16 [16384, 128], P('hid', 'dp')
- grad_down_right: bfloat16 [128, 8192], P('dp', 'hid')
All inputs are finite; a program needn't handle non-finite values.
Results may differ from a plain program's by a relative error of at most 0.022.
Values may be sent and summed in bfloat16 or wider, within the bound.
A program may use at most 64 MiB of HBM per device.

v0:
```python
import jax
import jax.numpy as jnp
from jax import lax
from jax.sharding import PartitionSpec as P

gelu_coef = 0.7978845608028654
cubic_coef = 0.044715


def from_partner(value, axis, distance):
    mask = 2**distance
    pairs = [(source, source ^ mask) for source in range(lax.axis_size(axis))]
    return lax.ppermute(value, axis, pairs)


def gelu_pair(pre_act):
    tangent = jnp.tanh(gelu_coef * (pre_act + cubic_coef * pre_act * pre_act * pre_act))
    activated = 0.5 * pre_act * (1.0 + tangent)
    derivative = 0.5 * (1.0 + tangent) + 0.5 * pre_act * (1.0 - tangent * tangent) * gelu_coef * (
        1.0 + 3.0 * cubic_coef * pre_act * pre_act
    )
    return (activated, derivative)


def per_device(
    inputs, out_grad, home_block, blocks_up, blocks_down, up_left, up_right, down_left, down_right
):
    single = jnp.float32
    half_type = jnp.bfloat16
    highest = lax.Precision.HIGHEST
    row_count, width_dev = inputs.shape
    hid_blocks, slot_count, shard_rows, blk_size = blocks_up.shape
    level_count = slot_count - 1
    in_blocks = width_dev // blk_size
    hidden_dev = hid_blocks * blk_size
    top_bit = lax.axis_size("hid").bit_length() - 1
    grad_scale = float(lax.axis_size("dp") * row_count) ** (-0.5)
    select = (home_block[:, None] == jnp.arange(in_blocks, dtype=jnp.int32)[None, :]).astype(single)
    full_up, full_down, left_in, right_in, left_out, right_out = (
        lax.all_gather(blocks_up, "dp", axis=2, tiled=True),
        lax.all_gather(blocks_down, "dp", axis=2, tiled=True),
        lax.all_gather(up_left, "dp", axis=1, tiled=True),
        lax.all_gather(up_right, "dp", axis=0, tiled=True),
        lax.all_gather(down_left, "dp", axis=1, tiled=True),
        lax.all_gather(down_right, "dp", axis=0, tiled=True),
    )
    rank_in = lax.psum(jnp.dot(inputs, left_in, preferred_element_type=single), "hid")
    rank_in = rank_in.astype(half_type)
    in_pieces = [inputs]
    grad_pieces = [out_grad]
    for level_idx in range(level_count):
        in_pieces.append(from_partner(inputs, "hid", top_bit - 1 - level_idx))

    def pick_blocks(pieces):
        stacked = jnp.stack(pieces, 0).reshape(slot_count, row_count, in_blocks, blk_size)
        return jnp.take(stacked, home_block, axis=2)

    picked = pick_blocks(in_pieces)
    part_rows = picked
    up_sum = jnp.einsum("sthk,hskn->thn", part_rows, full_up, preferred_element_type=single)
    pre_act = up_sum.reshape(row_count, hidden_dev) + jnp.dot(
        rank_in, right_in, preferred_element_type=single
    )
    activated, derivative = gelu_pair(pre_act)
    hidden = activated.astype(half_type)
    hidden_blocks = hidden.reshape(row_count, hid_blocks, blk_size)
    rank_mid = lax.psum(jnp.dot(hidden, left_out, preferred_element_type=single), "hid").astype(
        half_type
    )
    part_rows = hidden_blocks
    down_sum = jnp.einsum("thk,hskn->sthn", part_rows, full_down, preferred_element_type=single)
    placed = jnp.einsum("sthn,hi->stin", down_sum, select, precision=highest)
    total = placed[0]
    for level_idx in range(level_count):
        arrived = from_partner(placed[level_idx + 1], "hid", top_bit - 1 - level_idx)
        total = total + arrived
    outputs = (
        total.reshape(row_count, width_dev)
        + jnp.dot(rank_mid, right_out, preferred_element_type=single)
    ).astype(half_type)
    rank_back = lax.psum(jnp.dot(out_grad, right_out.T, preferred_element_type=single), "hid")
    rank_back = rank_back.astype(half_type)
    for level_idx in range(level_count):
        grad_pieces.append(from_partner(out_grad, "hid", top_bit - 1 - level_idx))
    grad_picked = pick_blocks(grad_pieces)
    grad_hidden = jnp.einsum(
        "sthn,hskn->thk", grad_picked, full_down, preferred_element_type=single
    )
    grad_pre = (
        (
            grad_hidden.reshape(row_count, hidden_dev)
            + jnp.dot(rank_back, left_out.T, preferred_element_type=single)
        )
        * derivative
    ).astype(half_type)
    rank_grad = lax.psum(
        jnp.dot(grad_pre, right_in.T, preferred_element_type=single), "hid"
    ).astype(half_type)
    grad_blocks = grad_pre.reshape(row_count, hid_blocks, blk_size)
    back_sum = jnp.einsum("thn,hskn->sthk", grad_blocks, full_up, preferred_element_type=single)
    back_placed = jnp.einsum("sthk,hi->stik", back_sum, select, precision=highest)
    back_total = back_placed[0]
    for level_idx in range(level_count):
        arrived = from_partner(back_placed[level_idx + 1], "hid", top_bit - 1 - level_idx)
        back_total = back_total + arrived
    input_grad = (
        back_total.reshape(row_count, width_dev)
        + jnp.dot(rank_grad, left_in.T, preferred_element_type=single)
    ).astype(half_type)
    summed = (
        lax.psum_scatter(
            (
                grad_scale
                * jnp.einsum("sthk,thn->hskn", picked, grad_blocks, preferred_element_type=single)
            ).astype(jnp.bfloat16),
            "dp",
            scatter_dimension=2,
            tiled=True,
        ).astype(jnp.float32),
        lax.psum_scatter(
            (
                grad_scale
                * jnp.einsum(
                    "thk,sthn->hskn", hidden_blocks, grad_picked, preferred_element_type=single
                )
            ).astype(jnp.bfloat16),
            "dp",
            scatter_dimension=2,
            tiled=True,
        ).astype(jnp.float32),
        lax.psum_scatter(
            (grad_scale * jnp.dot(inputs.T, rank_grad, preferred_element_type=single)).astype(
                jnp.bfloat16
            ),
            "dp",
            scatter_dimension=1,
            tiled=True,
        ).astype(jnp.float32),
        lax.psum_scatter(
            (grad_scale * jnp.dot(rank_in.T, grad_pre, preferred_element_type=single)).astype(
                jnp.bfloat16
            ),
            "dp",
            scatter_dimension=0,
            tiled=True,
        ).astype(jnp.float32),
        lax.psum_scatter(
            (grad_scale * jnp.dot(hidden.T, rank_back, preferred_element_type=single)).astype(
                jnp.bfloat16
            ),
            "dp",
            scatter_dimension=1,
            tiled=True,
        ).astype(jnp.float32),
        lax.psum_scatter(
            (grad_scale * jnp.dot(rank_mid.T, out_grad, preferred_element_type=single)).astype(
                jnp.bfloat16
            ),
            "dp",
            scatter_dimension=0,
            tiled=True,
        ).astype(jnp.float32),
    )
    return (outputs, input_grad) + tuple((summed_part.astype(half_type) for summed_part in summed))


def solution(mesh):
    placed = (
        P("dp", "hid"),
        P("dp", "hid"),
        P("hid"),
        P("hid", None, "dp", None),
        P("hid", None, "dp", None),
        P("hid", "dp"),
        P("dp", "hid"),
        P("hid", "dp"),
        P("dp", "hid"),
    )
    return jax.shard_map(
        per_device,
        mesh=mesh,
        in_specs=placed,
        out_specs=(
            P("dp", "hid"),
            P("dp", "hid"),
            P("hid", None, "dp", None),
            P("hid", None, "dp", None),
            P("hid", "dp"),
            P("dp", "hid"),
            P("hid", "dp"),
            P("dp", "hid"),
        ),
        check_vma=False,
    )
```

profile of v0, /device:TPU:8, one launch (start us, length us, event | category | flops | bytes accessed | tf_op | source)
XLA Modules:
  0.0 738.6 jit_solution(1994460682840392459)
XLA Ops:
  9.8 6.8 collective-permute-start
  16.7 2.7 collective-permute-start.1
  20.5 4.7 collective-permute-start.4
  25.2 2.2 collective-permute-start.5
  27.6 49.3 %all-gather = bf16[32,4,512]{2,1,0:T(4,128)(2,1)S(1)} all-gather(bf16[1,4,512]{2,1,0:T(4,128)(2,1)S(1)} %bitcast.138), channel_id=1, replica_groups=mesh['dp'=32,'hid'=16] {'dp'}, dimensions={0}, use_global_device_ids=true | all-gather | bytes 135168 | tf_op jit(solution)/shard_map/all_gather | solution.py:42
  77.2 42.4 %all-gather.3 = bf16[32,4,512]{2,1,0:T(4,128)(2,1)S(1)} all-gather(bf16[1,4,512]{2,1,0:T(4,128)(2,1)S(1)} %bitcast.139), channel_id=1, replica_groups=mesh['dp'=32,'hid'=16] {'dp'}, dimensions={0}, use_global_device_ids=true | all-gather | bytes 135168 | tf_op jit(solution)/shard_map/all_gather | solution.py:45
  119.9 46.7 %all-gather.1 = bf16[32,4,1024]{2,1,0:T(4,128)(2,1)S(1)} all-gather(bf16[1,4,1024]{2,1,0:T(4,128)(2,1)S(1)} %bitcast.136), channel_id=1, replica_groups=mesh['dp'=32,'hid'=16] {'dp'}, dimensions={0}, use_global_device_ids=true | all-gather | bytes 270336 | tf_op jit(solution)/shard_map/all_gather | solution.py:43
  167.6 45.5 %all-reduce.13 = (bf16[256,128]{1,0:T(8,128)(2,1)S(1)}, bf16[256,128]{1,0:T(8,128)(2,1)S(1)}) all-reduce(f32[256,128]{1,0:T(8,128)S(1)} %fusion.57, f32[256,128]{1,0:T(8,128)S(1)} %fusion.59), channel_id=1, replica_groups=mesh['dp'=32,'hid'=16] {'hid'}, use_global_device_ids=true, to_apply=%region_0.2 | all-reduce | flops 65536 | bytes 393216 | tf_op jit(solution)/shard_map/psum | solution.py:47
  213.1 48.1 %all-gather.2 = bf16[32,4,1024]{2,1,0:T(4,128)(2,1)S(1)} all-gather(bf16[1,4,1024]{2,1,0:T(4,128)(2,1)S(1)} %bitcast.137), channel_id=1, replica_groups=mesh['dp'=32,'hid'=16] {'dp'}, dimensions={0}, use_global_device_ids=true | all-gather | bytes 270336 | tf_op jit(solution)/shard_map/all_gather | solution.py:44
  264.7 1.8 pad_maximum_fusion.1
  266.5 1.9 gather_fusion.1
  268.4 3.2 fusion.8
  271.6 2.6 copy.60
  274.2 3.1 fusion.5
  277.4 2.7 copy.89
  285.1 48.0 %all-reduce.14 = (bf16[256,128]{1,0:T(8,128)(2,1)S(1)}, bf16[256,128]{1,0:T(8,128)(2,1)S(1)}) all-reduce(f32[256,128]{1,0:T(8,128)S(1)} %fusion.58, f32[256,128]{1,0:T(8,128)S(1)} %fusion.60), channel_id=1, replica_groups=mesh['dp'=32,'hid'=16] {'hid'}, use_global_device_ids=true, to_apply=%region_1.0 | all-reduce | flops 65536 | bytes 393216 | tf_op jit(solution)/shard_map/psum | solution.py:67
  334.8 2.3 fusion.10
  337.1 2.4 copy.76
  339.7 1.4 dynamic-slice
  343.7 1.4 copy.117
  345.0 2.9 reshape.97
  347.9 1.4 copy-done.3
  349.9 4.1 fusion.16
  354.4 7.7 %collective-permute-start.6 = (f32[256,2,256]{2,1,0:T(2,128)S(1)}, f32[256,2,256]{2,1,0:T(2,128)S(1)}, u32[]{:S(2)}, u32[]{:S(2)}) collective-permute-start(f32[256,2,256]{2,1,0:T(2,128)S(1)} %get-tuple-element.50), channel_id=1, source_target_pairs={{0,8},{1,9},{2,10},{3,11},{4,12},{5,13},{6,14},{7,15},{8,0},{9,1},... | collective-permute-start | bytes 1572872 | tf_op jit(solution)/shard_map/ppermute | solution.py:13
  362.1 1.9 collective-permute-start.7
  364.6 4.1 fusion.13
  369.1 7.0 collective-permute-start.2
  376.1 1.9 collective-permute-start.3
  378.4 62.6 %collective-permute-done.7 = f32[256,2,256]{2,1,0:T(2,128)S(1)} collective-permute-done((f32[256,2,256]{2,1,0:T(2,128)S(1)}, f32[256,2,256]{2,1,0:T(2,128)S(1)}, u32[]{:S(2)}, u32[]{:S(2)}) %collective-permute-start.7) | collective-permute-done | bytes 524320 | tf_op jit(solution)/shard_map/ppermute | solution.py:13
  441.4 10.7 %collective-permute-done.3 = f32[256,2,256]{2,1,0:T(2,128)S(1)} collective-permute-done((f32[256,2,256]{2,1,0:T(2,128)S(1)}, f32[256,2,256]{2,1,0:T(2,128)S(1)}, u32[]{:S(2)}, u32[]{:S(2)}) %collective-permute-start.3) | collective-permute-done | bytes 524320 | tf_op jit(solution)/shard_map/ppermute | solution.py:13
  453.5 52.5 %all-reduce.12.cloned.1.call-done = (bf16[4,3,256,256]{3,0,1,2:T(4,128)(2,1)}, bf16[512,128]{0,1:T(8,128)(2,1)}, bf16[128,1024]{1,0:T(8,128)(2,1)}, bf16[1024,128]{0,1:T(8,128)(2,1)}, bf16[128,512]{1,0:T(8,128)(2,1)}) async-done(((bf16[4,3,256,256]{3,0,1,2:T(4,128)(2,1)}, bf16[512,128]{0,1:T(8,128)(2,1)}, bf16[128,1024]{1,0:T(8,128)(2,1)}, bf16[1024,128]{0,1:T(8,128)(2,1)}, bf16[128,512]{1,0:T(8,128)(2,1)}), ...) | async-done | bytes 2359312
  512.6 218.0 %reduce-scatter.4.cloned.1.call-done = bf16[8,3072]{1,0:T(8,128)(2,1)} async-done(((bf16[256,3072]{1,0:T(8,128)(2,1)}), bf16[8,3072]{1,0:T(8,128)(2,1)}) %reduce-scatter.4.cloned.1.call-update) | async-done | bytes 49168
  (94 shorter events, 29.2 us)
Async XLA Ops:
  7.2 69.8 %copy-start.2 = (bf16[256,512]{1,0:T(8,128)(2,1)S(1)}, bf16[256,512]{1,0:T(8,128)(2,1)}, u32[]{:S(2)}) copy-start(bf16[256,512]{1,0:T(8,128)(2,1)} %param.11) | copy-start | bytes 786436
  7.2 112.5 %copy-start.1 = (bf16[256,512]{1,0:T(8,128)(2,1)S(1)}, bf16[256,512]{1,0:T(8,128)(2,1)}, u32[]{:S(2)}) copy-start(bf16[256,512]{1,0:T(8,128)(2,1)} %param.12) | copy-start | bytes 786436
  7.2 20.4 %copy-start.12 = (bf16[512,4]{0,1:T(4,128)(2,1)S(1)}, bf16[512,4]{0,1:T(4,128)(2,1)}, u32[]{:S(2)}) copy-start(bf16[512,4]{0,1:T(4,128)(2,1)} %param.16) | copy-start | bytes 12292
  7.2 70.0 %copy-start.13 = (bf16[4,512]{1,0:T(4,128)(2,1)S(1)}, bf16[4,512]{1,0:T(4,128)(2,1)}, u32[]{:S(2)}) copy-start(bf16[4,512]{1,0:T(4,128)(2,1)} %param.19) | copy-start | bytes 12292
  7.2 261.2 %all-gather.7.cloned.1.call-start = ((), (), s32[]{:S(2)}) async-start(), calls=%async_computation.1 | async-start | bytes 1622016 | tf_op jit(solution)/shard_map/all_gather | solution.py:40
  7.9 266.3 %all-gather.9.cloned.1.call-start = ((), (), s32[]{:S(2)}) async-start(), calls=%async_computation.2 | async-start | bytes 1622016 | tf_op jit(solution)/shard_map/all_gather | solution.py:41
  8.7 497.2 %all-reduce.12.cloned.1.call-start = ((), (), s32[]{:S(2)}) async-start(), calls=%async_computation.4 | async-start | bytes 4718592
  9.8 110.1 %copy-start.10 = (bf16[4,1024]{1,0:T(4,128)(2,1)S(1)}, bf16[4,1024]{1,0:T(4,128)(2,1)}, u32[]{:S(2)}) copy-start(bf16[4,1024]{1,0:T(4,128)(2,1)} %param.17) | copy-start | bytes 24580
  9.8 252.2 %collective-permute-start = (bf16[256,512]{0,1:T(8,128)(2,1)S(1)}, bf16[256,512]{0,1:T(8,128)(2,1)S(1)}, u32[]{:S(2)}, u32[]{:S(2)}) collective-permute-start(bf16[256,512]{0,1:T(8,128)(2,1)S(1)} %copy.54), channel_id=1, source_target_pairs={{0,8},{1,9},{2,10},{3,11},{4,12},{5,13},{6,14},{7,15},{8,0},{9,1},... | collective-permute-start | bytes 786440 | tf_op jit(solution)/shard_map/ppermute | solution.py:13
  16.7 245.5 %collective-permute-start.1 = (bf16[256,512]{0,1:T(8,128)(2,1)S(1)}, bf16[256,512]{0,1:T(8,128)(2,1)S(1)}, u32[]{:S(2)}, u32[]{:S(2)}) collective-permute-start(bf16[256,512]{0,1:T(8,128)(2,1)S(1)} %copy.54), channel_id=1, source_target_pairs={{0,4},{1,5},{2,6},{3,7},{4,0},{5,1},{6,2},{7,3},{8,12},{9,13},{10,... | collective-permute-start | bytes 786440 | tf_op jit(solution)/shard_map/ppermute | solution.py:13
  20.5 241.8 %collective-permute-start.4 = (bf16[256,512]{0,1:T(8,128)(2,1)S(1)}, bf16[256,512]{0,1:T(8,128)(2,1)S(1)}, u32[]{:S(2)}, u32[]{:S(2)}) collective-permute-start(bf16[256,512]{0,1:T(8,128)(2,1)S(1)} %copy.63), channel_id=1, source_target_pairs={{0,8},{1,9},{2,10},{3,11},{4,12},{5,13},{6,14},{7,15},{8,0},{9,1},... | collective-permute-start | bytes 786440 | tf_op jit(solution)/shard_map/ppermute | solution.py:13
  25.2 237.9 %collective-permute-start.5 = (bf16[256,512]{0,1:T(8,128)(2,1)S(1)}, bf16[256,512]{0,1:T(8,128)(2,1)S(1)}, u32[]{:S(2)}, u32[]{:S(2)}) collective-permute-start(bf16[256,512]{0,1:T(8,128)(2,1)S(1)} %copy.63), channel_id=1, source_target_pairs={{0,4},{1,5},{2,6},{3,7},{4,0},{5,1},{6,2},{7,3},{8,12},{9,13},{10,... | collective-permute-start | bytes 786440 | tf_op jit(solution)/shard_map/ppermute | solution.py:13
  27.6 139.9 %copy-start.14 = (s32[4]{0:T(128)S(1)}, s32[4]{0:T(128)}, u32[]{:S(2)}) copy-start(s32[4]{0:T(128)} %param.13) | copy-start | bytes 52
  77.0 136.1 %copy-start.11 = (bf16[1024,4]{0,1:T(4,128)(2,1)S(1)}, bf16[1024,4]{0,1:T(4,128)(2,1)}, u32[]{:S(2)}) copy-start(bf16[1024,4]{0,1:T(4,128)(2,1)} %param.18) | copy-start | bytes 24580
  264.7 3.6 copy-start.4
  271.6 2.7 copy-start.6
  277.4 2.7 copy-start.8
  280.1 0.9 copy-start.7
  280.1 1.3 copy-start.9
  339.5 3.3 copy-start.5
  339.5 391.1 %reduce-scatter.4.cloned.1.call-start = ((), (), s32[]{:S(2)}) async-start(), calls=%async_computation.3 | async-start | bytes 1622016
  347.9 1.4 copy-start.3
  354.0 10.0 %copy-start = (bf16[4,3,256,256]{3,2,1,0:T(8,128)(2,1)S(1)}, bf16[4,3,256,256]{3,2,1,0:T(8,128)(2,1)}, u32[]{:S(2)}) copy-start(bf16[4,3,256,256]{3,2,1,0:T(8,128)(2,1)} %all-gather.9.cloned.1.call-done) | copy-start | bytes 4718596
  354.4 24.0 %collective-permute-start.6 = (f32[256,2,256]{2,1,0:T(2,128)S(1)}, f32[256,2,256]{2,1,0:T(2,128)S(1)}, u32[]{:S(2)}, u32[]{:S(2)}) collective-permute-start(f32[256,2,256]{2,1,0:T(2,128)S(1)} %get-tuple-element.50), channel_id=1, source_target_pairs={{0,8},{1,9},{2,10},{3,11},{4,12},{5,13},{6,14},{7,15},{8,0},{9,1},... | collective-permute-start | bytes 1572872 | tf_op jit(solution)/shard_map/ppermute | solution.py:13
  362.1 78.9 %collective-permute-start.7 = (f32[256,2,256]{2,1,0:T(2,128)S(1)}, f32[256,2,256]{2,1,0:T(2,128)S(1)}, u32[]{:S(2)}, u32[]{:S(2)}) collective-permute-start(f32[256,2,256]{2,1,0:T(2,128)S(1)} %get-tuple-element.51), channel_id=1, source_target_pairs={{0,4},{1,5},{2,6},{3,7},{4,0},{5,1},{6,2},{7,3},{8,12},{9,13},{10,... | collective-permute-start | bytes 1572872 | tf_op jit(solution)/shard_map/ppermute | solution.py:13
  369.1 72.3 %collective-permute-start.2 = (f32[256,2,256]{2,1,0:T(2,128)S(1)}, f32[256,2,256]{2,1,0:T(2,128)S(1)}, u32[]{:S(2)}, u32[]{:S(2)}) collective-permute-start(f32[256,2,256]{2,1,0:T(2,128)S(1)} %get-tuple-element.52), channel_id=1, source_target_pairs={{0,8},{1,9},{2,10},{3,11},{4,12},{5,13},{6,14},{7,15},{8,0},{9,1},... | collective-permute-start | bytes 1572872 | tf_op jit(solution)/shard_map/ppermute | solution.py:13
  376.1 76.1 %collective-permute-start.3 = (f32[256,2,256]{2,1,0:T(2,128)S(1)}, f32[256,2,256]{2,1,0:T(2,128)S(1)}, u32[]{:S(2)}, u32[]{:S(2)}) collective-permute-start(f32[256,2,256]{2,1,0:T(2,128)S(1)} %get-tuple-element.53), channel_id=1, source_target_pairs={{0,4},{1,5},{2,6},{3,7},{4,0},{5,1},{6,2},{7,3},{8,12},{9,13},{10,... | collective-permute-start | bytes 1572872 | tf_op jit(solution)/shard_map/ppermute | solution.py:13
Sparse Core Ops, SparseCore 0:
  11.1 83.7 all-gather.6
  97.9 77.6 all-gather.8
  339.6 166.2 all-reduce.11
  510.8 219.7 reduce-scatter.3
where the time goes:
time: 740 us; the launch traced here: 739 us
  waiting for transfers between devices  345 us (47%)
  blocking collectives  280 us (38%)
  starting transfers between devices  35.3 us (5%)
  local copies, waits for them, and re-layouts  33.8 us (5%)
  matrix products  25.2 us (3%)
  between operations  15.6 us (2%)
    unnamed x6, waiting for transfers between devices  272 us
    ppermute x8, waiting for transfers between devices, from_partner(): return lax.ppermute(value, axis, pairs)  73.3 us
    all_gather x1, blocking collectives, per_device(): lax.all_gather(up_left, 'dp', axis=1, tiled=True)  49.3 us
    all_gather x1, blocking collectives, per_device(): lax.all_gather(down_left, 'dp', axis=1, tiled=True)  48.1 us
    psum x1, blocking collectives, per_device(): lax.psum(jnp.dot(hidden, left_out, preferred_element_type=single), 'hid')  48 us
    all_gather x1, blocking collectives, per_device(): lax.all_gather(up_right, 'dp', axis=0, tiled=True)  46.7 us
    psum x1, blocking collectives, per_device(): lax.psum(jnp.dot(inputs, left_in, preferred_element_type=single), 'hid')  45.5 us
    all_gather x1, blocking collectives, per_device(): lax.all_gather(down_right, 'dp', axis=0, tiled=True)  42.4 us
  transfers between devices with their start and end apart: 12, of which 4 were waited for; matrix products, arithmetic and copies ran while one was open for 6% of the time, Pallas kernels for 0%

commit v1 on v0

--- a/solution.py
+++ b/solution.py
@@ -5,6 +5,9 @@
 
 gelu_coef = 0.7978845608028654
 cubic_coef = 0.044715
+members_all_render = lambda z: jnp.concatenate(
+    jax.lax.all_to_all(jnp.stack([z] * jax.lax.axis_size("dp"), axis=0), "dp", 0, 0), 0
+)
 
 
 def from_partner(value, axis, distance):
@@ -40,7 +43,7 @@
         lax.all_gather(blocks_up, "dp", axis=2, tiled=True),
         lax.all_gather(blocks_down, "dp", axis=2, tiled=True),
         lax.all_gather(up_left, "dp", axis=1, tiled=True),
-        lax.all_gather(up_right, "dp", axis=0, tiled=True),
+        members_all_render(up_right),
         lax.all_gather(down_left, "dp", axis=1, tiled=True),
         lax.all_gather(down_right, "dp", axis=0, tiled=True),
     )

time: 740 us -> 704 us (0.951)
  blocking collectives: 280 us -> 228 us
  starting transfers between devices: 35.3 us -> 48.3 us
    all_gather x1 -> x0, blocking collectives: 46.7 us -> none  [per_device(): lax.all_gather(up_right, 'dp', axis=0, tiled=True)]
    all_to_all x0 -> x1, starting transfers between devices: none -> 13.3 us  [jax.lax.all_to_all(jnp.stack([z] * jax.lax.axis_size('dp'), axis=0), 'dp'...]
    unnamed x49 -> x44, local copies, waits for them, and re-layouts: 19.2 us -> 18.4 us
  transfers between devices with their start and end apart: 12 -> 13, of which waited for: 4 -> 4; matrix products, arithmetic and copies ran while one was open for 6% -> 6% of each run, Pallas kernels for 0% -> 0%
where the time goes in v1:
time: 704 us; the launch traced here: 703 us
  waiting for transfers between devices  348 us (49%)
  blocking collectives  228 us (32%)
  starting transfers between devices  48.3 us (7%)
  local copies, waits for them, and re-layouts  35.5 us (5%)
  matrix products  25.2 us (4%)
  between operations  15.6 us (2%)
    unnamed x6, waiting for transfers between devices  274 us
    ppermute x8, waiting for transfers between devices, from_partner(): return lax.ppermute(value, axis, pairs)  73.2 us
    psum x1, blocking collectives, per_device(): lax.psum(jnp.dot(hidden, left_out, preferred_element_type=single), 'hid')  47.9 us
    all_gather x1, blocking collectives, per_device(): lax.all_gather(down_left, 'dp', axis=1, tiled=True)  47.8 us
    psum x1, blocking collectives, per_device(): lax.psum(jnp.dot(inputs, left_in, preferred_element_type=single), 'hid')  46.1 us
    all_gather x1, blocking collectives, per_device(): lax.all_gather(up_left, 'dp', axis=1, tiled=True)  43.9 us
    all_gather x1, blocking collectives, per_device(): lax.all_gather(down_right, 'dp', axis=0, tiled=True)  41.8 us
    ppermute x8, starting transfers between devices, from_partner(): return lax.ppermute(value, axis, pairs)  34.7 us
  transfers between devices with their start and end apart: 13, of which 4 were waited for; matrix products, arithmetic and copies ran while one was open for 6% of the time, Pallas kernels for 0%

profile of v1, /device:TPU:8, one launch (start us, length us, event | category | flops | bytes accessed | tf_op | source)
XLA Modules:
  0.0 703.2 jit_solution(16605383848177542700)
XLA Ops:
  9.8 6.8 collective-permute-start
  16.7 2.7 collective-permute-start.1
  20.5 4.7 collective-permute-start.4
  25.2 2.2 collective-permute-start.5
  27.5 1.5 stack.22
  28.9 13.3 %all-to-all-start = ((bf16[32,4,1024]{2,1,0:T(4,128)(2,1)}), bf16[32,4,1024]{2,1,0:T(4,128)(2,1)}, u32[]{:S(2)}, u32[]{:S(2)}) async-start(bf16[32,4,1024]{2,1,0:T(4,128)(2,1)} %stack.22), calls=%async_computation | async-start | bytes 524288 | tf_op jit(solution)/shard_map/all_to_all | solution.py:9
  42.3 43.9 %all-gather = bf16[32,4,512]{2,1,0:T(4,128)(2,1)S(1)} all-gather(bf16[1,4,512]{2,1,0:T(4,128)(2,1)S(1)} %bitcast.136), channel_id=1, replica_groups=mesh['dp'=32,'hid'=16] {'dp'}, dimensions={0}, use_global_device_ids=true | all-gather | bytes 135168 | tf_op jit(solution)/shard_map/all_gather | solution.py:45
  86.5 41.8 %all-gather.2 = bf16[32,4,512]{2,1,0:T(4,128)(2,1)S(1)} all-gather(bf16[1,4,512]{2,1,0:T(4,128)(2,1)S(1)} %bitcast.137), channel_id=1, replica_groups=mesh['dp'=32,'hid'=16] {'dp'}, dimensions={0}, use_global_device_ids=true | all-gather | bytes 135168 | tf_op jit(solution)/shard_map/all_gather | solution.py:48
  128.6 46.1 %all-reduce.13 = (bf16[256,128]{1,0:T(8,128)(2,1)S(1)}, bf16[256,128]{1,0:T(8,128)(2,1)S(1)}) all-reduce(f32[256,128]{1,0:T(8,128)S(1)} %fusion.57, f32[256,128]{1,0:T(8,128)S(1)} %fusion.59), channel_id=1, replica_groups=mesh['dp'=32,'hid'=16] {'hid'}, use_global_device_ids=true, to_apply=%region_0.2 | all-reduce | flops 65536 | bytes 393216 | tf_op jit(solution)/shard_map/psum | solution.py:50
  174.7 47.8 %all-gather.1 = bf16[32,4,1024]{2,1,0:T(4,128)(2,1)S(1)} all-gather(bf16[1,4,1024]{2,1,0:T(4,128)(2,1)S(1)} %bitcast.135), channel_id=1, replica_groups=mesh['dp'=32,'hid'=16] {'dp'}, dimensions={0}, use_global_device_ids=true | all-gather | bytes 270336 | tf_op jit(solution)/shard_map/all_gather | solution.py:47
  226.4 1.8 pad_maximum_fusion.1
  228.2 1.9 gather_fusion.1
  231.1 3.2 fusion.8
  234.3 2.6 copy.60
  236.9 3.1 fusion.5
  240.1 2.7 copy.89
  247.7 47.9 %all-reduce.14 = (bf16[256,128]{1,0:T(8,128)(2,1)S(1)}, bf16[256,128]{1,0:T(8,128)(2,1)S(1)}) all-reduce(f32[256,128]{1,0:T(8,128)S(1)} %fusion.58, f32[256,128]{1,0:T(8,128)S(1)} %fusion.60), channel_id=1, replica_groups=mesh['dp'=32,'hid'=16] {'hid'}, use_global_device_ids=true, to_apply=%region_1.0 | all-reduce | flops 65536 | bytes 393216 | tf_op jit(solution)/shard_map/psum | solution.py:70
  297.4 2.3 fusion.10
  299.7 2.4 copy.76
  302.3 1.4 dynamic-slice
  307.6 2.9 reshape.101
  310.5 1.4 copy-done.3
  312.5 4.1 fusion.16
  317.0 7.3 %collective-permute-start.6 = (f32[256,2,256]{2,1,0:T(2,128)S(1)}, f32[256,2,256]{2,1,0:T(2,128)S(1)}, u32[]{:S(2)}, u32[]{:S(2)}) collective-permute-start(f32[256,2,256]{2,1,0:T(2,128)S(1)} %get-tuple-element.50), channel_id=1, source_target_pairs={{0,8},{1,9},{2,10},{3,11},{4,12},{5,13},{6,14},{7,15},{8,0},{9,1},... | collective-permute-start | bytes 1572872 | tf_op jit(solution)/shard_map/ppermute | solution.py:16
  324.3 1.9 collective-permute-start.7
  326.8 4.1 fusion.13
  331.3 7.0 collective-permute-start.2
  338.3 1.9 collective-permute-start.3
  340.7 62.5 %collective-permute-done.7 = f32[256,2,256]{2,1,0:T(2,128)S(1)} collective-permute-done((f32[256,2,256]{2,1,0:T(2,128)S(1)}, f32[256,2,256]{2,1,0:T(2,128)S(1)}, u32[]{:S(2)}, u32[]{:S(2)}) %collective-permute-start.7) | collective-permute-done | bytes 524320 | tf_op jit(solution)/shard_map/ppermute | solution.py:16
  403.6 10.8 %collective-permute-done.3 = f32[256,2,256]{2,1,0:T(2,128)S(1)} collective-permute-done((f32[256,2,256]{2,1,0:T(2,128)S(1)}, f32[256,2,256]{2,1,0:T(2,128)S(1)}, u32[]{:S(2)}, u32[]{:S(2)}) %collective-permute-start.3) | collective-permute-done | bytes 524320 | tf_op jit(solution)/shard_map/ppermute | solution.py:16
  415.7 54.9 %all-reduce.12.cloned.1.call-done = (bf16[4,3,256,256]{3,0,1,2:T(4,128)(2,1)}, bf16[512,128]{0,1:T(8,128)(2,1)}, bf16[128,1024]{1,0:T(8,128)(2,1)}, bf16[1024,128]{0,1:T(8,128)(2,1)}, bf16[128,512]{1,0:T(8,128)(2,1)}) async-done(((bf16[4,3,256,256]{3,0,1,2:T(4,128)(2,1)}, bf16[512,128]{0,1:T(8,128)(2,1)}, bf16[128,1024]{1,0:T(8,128)(2,1)}, bf16[1024,128]{0,1:T(8,128)(2,1)}, bf16[128,512]{1,0:T(8,128)(2,1)}), ...) | async-done | bytes 2359312
  477.2 218.0 %reduce-scatter.4.cloned.1.call-done = bf16[8,3072]{1,0:T(8,128)(2,1)} async-done(((bf16[256,3072]{1,0:T(8,128)(2,1)}), bf16[8,3072]{1,0:T(8,128)(2,1)}) %reduce-scatter.4.cloned.1.call-update) | async-done | bytes 49168
  (92 shorter events, 30.8 us)
Async XLA Ops:
  7.2 79.1 %copy-start.2 = (bf16[256,512]{1,0:T(8,128)(2,1)S(1)}, bf16[256,512]{1,0:T(8,128)(2,1)}, u32[]{:S(2)}) copy-start(bf16[256,512]{1,0:T(8,128)(2,1)} %param.11) | copy-start | bytes 786436
  7.2 35.1 %copy-start.10 = (bf16[512,4]{0,1:T(4,128)(2,1)S(1)}, bf16[512,4]{0,1:T(4,128)(2,1)}, u32[]{:S(2)}) copy-start(bf16[512,4]{0,1:T(4,128)(2,1)} %param.16) | copy-start | bytes 12292
  7.2 79.3 %copy-start.11 = (bf16[4,512]{1,0:T(4,128)(2,1)S(1)}, bf16[4,512]{1,0:T(4,128)(2,1)}, u32[]{:S(2)}) copy-start(bf16[4,512]{1,0:T(4,128)(2,1)} %param.19) | copy-start | bytes 12292
  7.2 223.9 %all-gather.6.cloned.1.call-start = ((), (), s32[]{:S(2)}) async-start(), calls=%async_computation.2 | async-start | bytes 1622016 | tf_op jit(solution)/shard_map/all_gather | solution.py:43
  7.9 229.0 %all-gather.8.cloned.1.call-start = ((), (), s32[]{:S(2)}) async-start(), calls=%async_computation.3 | async-start | bytes 1622016 | tf_op jit(solution)/shard_map/all_gather | solution.py:44
  8.7 119.7 %copy-start.1 = (bf16[256,512]{1,0:T(8,128)(2,1)S(1)}, bf16[256,512]{1,0:T(8,128)(2,1)}, u32[]{:S(2)}) copy-start(bf16[256,512]{1,0:T(8,128)(2,1)} %param.12) | copy-start | bytes 786436
  9.8 118.8 %copy-start.12 = (s32[4]{0:T(128)S(1)}, s32[4]{0:T(128)}, u32[]{:S(2)}) copy-start(s32[4]{0:T(128)} %param.13) | copy-start | bytes 52
  9.8 213.8 %collective-permute-start = (bf16[256,512]{0,1:T(8,128)(2,1)S(1)}, bf16[256,512]{0,1:T(8,128)(2,1)S(1)}, u32[]{:S(2)}, u32[]{:S(2)}) collective-permute-start(bf16[256,512]{0,1:T(8,128)(2,1)S(1)} %copy.54), channel_id=1, source_target_pairs={{0,8},{1,9},{2,10},{3,11},{4,12},{5,13},{6,14},{7,15},{8,0},{9,1},... | collective-permute-start | bytes 786440 | tf_op jit(solution)/shard_map/ppermute | solution.py:16
  16.7 207.1 %collective-permute-start.1 = (bf16[256,512]{0,1:T(8,128)(2,1)S(1)}, bf16[256,512]{0,1:T(8,128)(2,1)S(1)}, u32[]{:S(2)}, u32[]{:S(2)}) collective-permute-start(bf16[256,512]{0,1:T(8,128)(2,1)S(1)} %copy.54), channel_id=1, source_target_pairs={{0,4},{1,5},{2,6},{3,7},{4,0},{5,1},{6,2},{7,3},{8,12},{9,13},{10,... | collective-permute-start | bytes 786440 | tf_op jit(solution)/shard_map/ppermute | solution.py:16
  20.5 154.3 %copy-start.9 = (bf16[1024,4]{0,1:T(4,128)(2,1)S(1)}, bf16[1024,4]{0,1:T(4,128)(2,1)}, u32[]{:S(2)}) copy-start(bf16[1024,4]{0,1:T(4,128)(2,1)} %param.18) | copy-start | bytes 24580
  20.5 203.4 %collective-permute-start.4 = (bf16[256,512]{0,1:T(8,128)(2,1)S(1)}, bf16[256,512]{0,1:T(8,128)(2,1)S(1)}, u32[]{:S(2)}, u32[]{:S(2)}) collective-permute-start(bf16[256,512]{0,1:T(8,128)(2,1)S(1)} %copy.63), channel_id=1, source_target_pairs={{0,8},{1,9},{2,10},{3,11},{4,12},{5,13},{6,14},{7,15},{8,0},{9,1},... | collective-permute-start | bytes 786440 | tf_op jit(solution)/shard_map/ppermute | solution.py:16
  25.2 199.6 %collective-permute-start.5 = (bf16[256,512]{0,1:T(8,128)(2,1)S(1)}, bf16[256,512]{0,1:T(8,128)(2,1)S(1)}, u32[]{:S(2)}, u32[]{:S(2)}) collective-permute-start(bf16[256,512]{0,1:T(8,128)(2,1)S(1)} %copy.63), channel_id=1, source_target_pairs={{0,4},{1,5},{2,6},{3,7},{4,0},{5,1},{6,2},{7,3},{8,12},{9,13},{10,... | collective-permute-start | bytes 786440 | tf_op jit(solution)/shard_map/ppermute | solution.py:16
  28.9 201.1 %all-to-all-start = ((bf16[32,4,1024]{2,1,0:T(4,128)(2,1)}), bf16[32,4,1024]{2,1,0:T(4,128)(2,1)}, u32[]{:S(2)}, u32[]{:S(2)}) async-start(bf16[32,4,1024]{2,1,0:T(4,128)(2,1)} %stack.22), calls=%async_computation | async-start | bytes 524288 | tf_op jit(solution)/shard_map/all_to_all | solution.py:9
  42.2 428.3 %all-reduce.12.cloned.1.call-start = ((), (), s32[]{:S(2)}) async-start(), calls=%async_computation.5 | async-start | bytes 4718592
  226.4 4.7 copy-start.4
  234.3 2.7 copy-start.6
  240.1 2.7 copy-start.7
  242.8 1.2 copy-start.8
  302.0 3.3 copy-start.5
  302.1 393.1 %reduce-scatter.4.cloned.1.call-start = ((), (), s32[]{:S(2)}) async-start(), calls=%async_computation.4 | async-start | bytes 1622016
  310.5 1.4 copy-start.3
  316.6 9.7 %copy-start = (bf16[4,3,256,256]{3,2,1,0:T(8,128)(2,1)S(1)}, bf16[4,3,256,256]{3,2,1,0:T(8,128)(2,1)}, u32[]{:S(2)}) copy-start(bf16[4,3,256,256]{3,2,1,0:T(8,128)(2,1)} %all-gather.8.cloned.1.call-done) | copy-start | bytes 4718596
  317.0 23.7 %collective-permute-start.6 = (f32[256,2,256]{2,1,0:T(2,128)S(1)}, f32[256,2,256]{2,1,0:T(2,128)S(1)}, u32[]{:S(2)}, u32[]{:S(2)}) collective-permute-start(f32[256,2,256]{2,1,0:T(2,128)S(1)} %get-tuple-element.50), channel_id=1, source_target_pairs={{0,8},{1,9},{2,10},{3,11},{4,12},{5,13},{6,14},{7,15},{8,0},{9,1},... | collective-permute-start | bytes 1572872 | tf_op jit(solution)/shard_map/ppermute | solution.py:16
  324.3 78.8 %collective-permute-start.7 = (f32[256,2,256]{2,1,0:T(2,128)S(1)}, f32[256,2,256]{2,1,0:T(2,128)S(1)}, u32[]{:S(2)}, u32[]{:S(2)}) collective-permute-start(f32[256,2,256]{2,1,0:T(2,128)S(1)} %get-tuple-element.51), channel_id=1, source_target_pairs={{0,4},{1,5},{2,6},{3,7},{4,0},{5,1},{6,2},{7,3},{8,12},{9,13},{10,... | collective-permute-start | bytes 1572872 | tf_op jit(solution)/shard_map/ppermute | solution.py:16
  331.3 72.2 %collective-permute-start.2 = (f32[256,2,256]{2,1,0:T(2,128)S(1)}, f32[256,2,256]{2,1,0:T(2,128)S(1)}, u32[]{:S(2)}, u32[]{:S(2)}) collective-permute-start(f32[256,2,256]{2,1,0:T(2,128)S(1)} %get-tuple-element.52), channel_id=1, source_target_pairs={{0,8},{1,9},{2,10},{3,11},{4,12},{5,13},{6,14},{7,15},{8,0},{9,1},... | collective-permute-start | bytes 1572872 | tf_op jit(solution)/shard_map/ppermute | solution.py:16
  338.3 76.0 %collective-permute-start.3 = (f32[256,2,256]{2,1,0:T(2,128)S(1)}, f32[256,2,256]{2,1,0:T(2,128)S(1)}, u32[]{:S(2)}, u32[]{:S(2)}) collective-permute-start(f32[256,2,256]{2,1,0:T(2,128)S(1)} %get-tuple-element.53), channel_id=1, source_target_pairs={{0,4},{1,5},{2,6},{3,7},{4,0},{5,1},{6,2},{7,3},{8,12},{9,13},{10,... | collective-permute-start | bytes 1572872 | tf_op jit(solution)/shard_map/ppermute | solution.py:16
Sparse Core Ops, SparseCore 0:
  11.1 85.1 all-gather.5
  99.3 77.2 all-gather.7
  302.2 168.3 all-reduce.11
  475.4 219.7 reduce-scatter.3
